TPU v7x, 32 devices: a whole 2x2x4 slice. The times are simulated.
32 devices in a mesh: ctx: 2 (over x), head: 4 (over y, core), rep: 4 (over z).
Axes of the slice: x: 2, y: 2, z: 4, core: 2. Of those that a mesh axis runs over, the one named last changes fastest.
Arguments:
- kv_cache: float32 [8, 2, 512, 8, 128], P('head', None, 'ctx', 'rep'), may hold values from -8 to 8
- prefill_q: float32 [8, 256, 64, 128], P('head', 'ctx', 'rep'), may hold values from -512 to 512
- decode_q: float32 [8, 8, 4, 64, 128], P(None, ('ctx', 'rep'), None, 'head'), may hold values from -512 to 512
- decode_kv: float32 [8, 8, 4, 2, 8, 128], P(None, ('ctx', 'rep'), None, None, 'head'), may hold values from -12 to 12
- lengths: int32 [8], replicated, may hold values from 256 to 512, as said below
- row_length: int32 [8, 8], P(None, ('ctx', 'rep')), may hold values from 2 to 512, as said below
Outputs:
- prefill_out: float32 [8, 256, 64, 128], P('head', 'ctx', 'rep')
- decode_out: float32 [8, 8, 4, 64, 128], P(None, ('ctx', 'rep'), None, 'head')
Inputs may be any that keep to these rules, and one draw needn't show every extreme that they name: `lengths`: multiples of 128; some request has length 512. `row_length`: a row reads at most its request's length; every request has a row that reads its whole length.
All inputs are finite; a program needn't handle non-finite values.
Results may differ from a plain program's by a relative error of at most 0.0003.
Values sent between devices are 32-bit elements; how exact they have to be, the bound alone decides.
No kernel may reach another device: no remote copies, remote signals or barrier semaphores. Data moves between devices by JAX's collectives and lax.ppermute only.
A program may use at most 128 MiB of HBM per device.

v0:
```python
import math
import jax
import jax.numpy as jnp
from jax import lax
from jax.sharding import PartitionSpec as P

NEG_FILL = -1e30
HIGH_PRECISION = lax.Precision.HIGHEST


def broadcast(value, axis, source):
    kept = jnp.where(lax.axis_index(axis) == source, value, 0).astype(value.dtype)
    return lax.psum(kept, axis)


def online_fold(running, scores, value_rows, pattern):
    run_max, run_total, run_acc = running
    new_max = jnp.maximum(run_max, jnp.max(scores, axis=-1))
    weights = jnp.exp(scores - new_max[..., None])
    new_total = jnp.sum(weights, axis=-1)
    new_acc = jnp.einsum(pattern, weights, value_rows, precision=HIGH_PRECISION)
    return (new_max, new_total, new_acc)


def empty_state(lead_shape, head_dim):
    return (
        jnp.full(lead_shape, NEG_FILL, jnp.float32),
        jnp.zeros(lead_shape, jnp.float32),
        jnp.zeros(lead_shape + (head_dim,), jnp.float32),
    )


def block_fold(running, query_rows, key_block, first_pos, limits, score_scale, strict):
    block_len = key_block.shape[2]
    scores = (
        jnp.einsum("bkrd,bnkd->bkrn", query_rows, key_block[:, 0], precision=HIGH_PRECISION)
        * score_scale
    )
    positions = first_pos + jnp.arange(block_len, dtype=jnp.int32)
    if strict:
        allowed = positions[None, None, :] < limits[:, :, None]
    else:
        allowed = positions[None, None, :] <= limits[:, :, None]
    scores = jnp.where(allowed[:, None], scores, NEG_FILL)
    return online_fold(running, scores, key_block[:, 1], "bkrn,bnkd->bkrd")


def source_major(values, slot_count, kv_heads, sources, count_rows, step_count, group_size):
    tail_shape = values.shape[3:]
    spread_out = values.reshape(
        (slot_count, kv_heads, sources, count_rows, step_count, group_size) + tail_shape
    )
    axes_order = (2, 0, 3, 4, 1, 5) + tuple(range(6, 6 + len(tail_shape)))
    moved = jnp.transpose(spread_out, axes_order)
    return moved.reshape(
        (sources, slot_count, count_rows, step_count, kv_heads * group_size) + tail_shape
    )


def on_device(kv_cache, prefill_q, decode_q, decode_kv, lengths, row_length):
    ctx_count = lax.axis_size("ctx")
    ctx_index = lax.axis_index("ctx")
    head_index = lax.axis_index("head")
    req_group, span_rows, rep_heads, head_dim = prefill_q.shape
    rep_kv = kv_cache.shape[3]
    group_size = rep_heads // rep_kv
    block_len = kv_cache.shape[2]
    score_scale = 1.0 / math.sqrt(head_dim)
    group_lengths = lax.dynamic_slice_in_dim(lengths, head_index * req_group, req_group)
    span_pos = (
        group_lengths[:, None]
        - span_rows * ctx_count
        + ctx_index * span_rows
        + jnp.arange(span_rows, dtype=jnp.int32)[None, :]
    )
    row_pos = jnp.repeat(span_pos, group_size, axis=1)
    prefill_rows = jnp.transpose(
        prefill_q.reshape(req_group, span_rows, rep_kv, group_size, head_dim), (0, 2, 1, 3, 4)
    ).reshape(req_group, rep_kv, span_rows * group_size, head_dim)
    start_state = empty_state((req_group, rep_kv, span_rows * group_size), head_dim)
    run_max, run_total, run_acc = block_fold(
        start_state,
        prefill_rows,
        lax.all_gather(kv_cache, "ctx", axis=2, tiled=True),
        jnp.int32(0),
        row_pos,
        score_scale,
        False,
    )
    prefill_vals = run_acc / run_total[..., None]
    prefill_out = jnp.transpose(
        prefill_vals.reshape(req_group, rep_kv, span_rows, group_size, head_dim), (0, 2, 1, 3, 4)
    ).reshape(prefill_q.shape)
    all_requests = lax.all_gather(kv_cache, "head", axis=0, tiled=True)
    head_cache = broadcast(all_requests, "rep", head_index)
    requests, row_count, step_count, local_heads, unused_dim = decode_q.shape
    kv_heads = local_heads // group_size
    gathered_rows, gathered_limits = (
        lax.all_gather(decode_q, "ctx", axis=1, tiled=True),
        lax.all_gather(row_length, "ctx", axis=1, tiled=True),
    )
    total_rows = gathered_rows.shape[1]
    grouped = jnp.transpose(
        gathered_rows.reshape(requests, total_rows, step_count, kv_heads, group_size, head_dim),
        (0, 3, 1, 2, 4, 5),
    ).reshape(requests, kv_heads, -1, head_dim)
    limits = jnp.broadcast_to(
        gathered_limits[:, :, None, None], (requests, total_rows, step_count, group_size)
    ).reshape(requests, -1)
    running = empty_state((requests, kv_heads, grouped.shape[2]), head_dim)
    running = block_fold(
        running, grouped, head_cache, ctx_index * block_len, limits, score_scale, True
    )
    shaped = tuple(
        (
            source_major(values, requests, kv_heads, ctx_count, row_count, step_count, group_size)
            for values in running
        )
    )
    home_max, home_total, home_acc = (
        lax.all_to_all(shaped[0], "ctx", split_axis=0, concat_axis=0, tiled=True),
        lax.all_to_all(shaped[1], "ctx", split_axis=0, concat_axis=0, tiled=True),
        lax.all_to_all(shaped[2], "ctx", split_axis=0, concat_axis=0, tiled=True),
    )
    ctx_max = jnp.max(home_max, axis=0)
    factor = jnp.exp(home_max - ctx_max[None])
    ctx_total = jnp.sum(home_total * factor, axis=0)
    ctx_acc = jnp.sum(home_acc * factor[..., None], axis=0)
    home_rows = decode_q.reshape(requests, row_count, step_count, kv_heads, group_size, head_dim)
    draft_scores = (
        jnp.einsum(
            "artkgd,arskd->artkgs", home_rows, decode_kv[:, :, :, 0], precision=HIGH_PRECISION
        )
        * score_scale
    )
    step_ids = jnp.arange(step_count, dtype=jnp.int32)
    causal = step_ids[None, :] <= step_ids[:, None]
    draft_scores = jnp.where(causal[None, None, :, None, None, :], draft_scores, NEG_FILL)
    ctx_max = ctx_max.reshape(requests, row_count, step_count, kv_heads, group_size)
    ctx_total = ctx_total.reshape(requests, row_count, step_count, kv_heads, group_size)
    ctx_acc = ctx_acc.reshape(requests, row_count, step_count, kv_heads, group_size, head_dim)
    joint_max = jnp.maximum(ctx_max, jnp.max(draft_scores, axis=-1))
    draft_weights = jnp.exp(draft_scores - joint_max[..., None])
    ctx_factor = jnp.exp(ctx_max - joint_max)
    denominator = ctx_total * ctx_factor + jnp.sum(draft_weights, axis=-1)
    numerator = ctx_acc * ctx_factor[..., None] + jnp.einsum(
        "artkgs,arskd->artkgd", draft_weights, decode_kv[:, :, :, 1], precision=HIGH_PRECISION
    )
    decode_out = (numerator / denominator[..., None]).reshape(decode_q.shape)
    return (prefill_out, decode_out)


def solution(mesh):
    in_specs = (
        P("head", None, "ctx", "rep", None),
        P("head", "ctx", "rep", None),
        P(None, ("ctx", "rep"), None, "head", None),
        P(None, ("ctx", "rep"), None, None, "head", None),
        P(),
        P(None, ("ctx", "rep")),
    )
    out_specs = (P("head", "ctx", "rep", None), P(None, ("ctx", "rep"), None, "head", None))
    return jax.shard_map(
        on_device, mesh=mesh, in_specs=in_specs, out_specs=out_specs, check_vma=False
    )
```

profile of v0, /device:TPU:0, one launch (start us, length us, event | category | flops | bytes accessed | tf_op | source)
XLA Modules:
  0.0 285.3 jit_solution(5755422686790085839)
XLA Ops:
  7.2 2.4 copy.82
  9.7 0.7 all-gather.4.cloned.1.call-update
  10.5 36.9 %all-gather.6.cloned.1.call-done = f32[8,2,256,2,128]{4,2,3,0,1:T(8,128)} async-done(((f32[2,2,256,2,128]{4,2,3,0,1:T(8,128)}), f32[8,2,256,2,128]{4,2,3,0,1:T(8,128)}) %all-gather.6.cloned.1.call-update) | async-done | bytes 4194320 | tf_op jit(solution)/shard_map/all_gather | solution.py:94
  47.4 4.6 %broadcast_select_fusion = f32[8,2,256,2,128]{4,2,3,0,1:T(8,128)} fusion(f32[8,2,256,2,128]{4,2,3,0,1:T(8,128)} %all-gather.6.cloned.1.call-done, pred[]{:T(512)S(6)} %eq.3), kind=kLoop, calls=%fused_computation.18 | loop fusion | flops 1048576 | bytes 8388609 | tf_op jit(solution)/shard_map/jit(_where)/select_n | solution.py:12
  52.0 0.6 copy-done.5
  52.6 4.2 %all-gather = s32[2,1,8]{2,1,0:T(1,128)S(1)} all-gather(s32[1,1,8]{2,1,0:T(1,128)S(1)} %bitcast.147), channel_id=1, replica_groups=mesh['ctx'=2,'head'=4,'rep'=4] {'ctx'}, dimensions={0}, use_global_device_ids=true | all-gather | bytes 96 | tf_op jit(solution)/shard_map/all_gather | solution.py:100
  56.8 0.1 copy.85
  57.0 0.1 lt.24
  57.1 0.1 add_add_fusion
  57.2 0.1 broadcast_in_dim.48
  57.3 0.1 le.37
  57.5 12.6 %all_gather.15 = f32[8,2,4,16,128]{4,3,2,1,0:T(8,128)S(1)} all-gather(f32[8,1,4,16,128]{4,3,2,1,0:T(8,128)S(1)} %copy-done.1), channel_id=1, replica_groups=mesh['ctx'=2,'head'=4,'rep'=4] {'ctx'}, dimensions={1}, use_global_device_ids=true | all-gather | bytes 786432 | tf_op jit(solution)/shard_map/all_gather | solution.py:99
  70.0 0.9 copy.87
  71.0 0.1 broadcast_compare_fusion
  71.1 3.6 %fusion.31 = (f32[8,4,2,8]{3,1,2,0:T(4,128)S(1)}, f32[8,1,4,2,8,4]{4,5,2,3,0,1:T(4,128)S(1)}) fusion(f32[8,1,4,1,2,128]{5,4,3,2,1,0:T(2,128)S(1)} %get-tuple-element.13, pred[4,4]{1,0:T(4,128)(4,1)S(1)} %iota_compare_fusion.1, f32[8,1,4,16,128]{4,3,2,1,0:T(8,128)S(1)} %copy-done.1), kind=kOutput, calls=%fused_computation.63 | convolution fusion | flops 3151360 | bytes 305168 | tf_op jit(solution)/shard_map/artkgd,arskd->artkgs/dot_general | solution.py:131
  74.7 0.6 iota_compare_fusion
  75.3 10.6 %all-gather.4.cloned.1.call-done = f32[2,2,512,2,128]{4,2,3,0,1:T(8,128)} async-done(((f32[2,2,256,2,128]{4,2,3,0,1:T(8,128)}), f32[2,2,512,2,128]{4,2,3,0,1:T(8,128)}) %all-gather.4.cloned.1.call-update) | async-done | bytes 2097168 | tf_op jit(solution)/shard_map/all_gather | solution.py:84
  86.0 9.6 %fusion = (f32[2,2,1024]{2,1,0:T(2,128)S(1)}, f32[2,2,1024,512]{2,3,1,0:T(8,128)S(1)}) fusion(pred[2,1024,512]{1,2,0:T(8,128)(4,1)S(1)} %iota_compare_fusion, f32[2,2,512,2,128]{4,2,3,0,1:T(8,128)} %all-gather.4.cloned.1.call-done, f32[2,128,16,128]{3,2,1,0:T(8,128)S(1)} %copy-done), kind=kOutput, calls=%fused_computation.2 | convolution fusion | flops 3227512832 | bytes 12599296 | tf_op jit(solution)/shard_map/bkrd,bnkd->bkrn/dot_general | solution.py:36
  95.6 2.2 fusion.1
  97.8 15.4 %divide_bitcast_fusion = f32[2,128,2,8,128]{4,3,1,2,0:T(8,128)S(1)} fusion(f32[2,2,1024]{2,1,0:T(2,128)S(1)} %fusion.1, f32[2,2,512,2,128]{4,2,3,0,1:T(8,128)S(1)} %copy-done.2, f32[2,2,1024,512]{2,3,1,0:T(8,128)S(1)} %get-tuple-element.17, f32[2,2,1024]{2,1,0:T(2,128)S(1)} %broadcast_maximum_fusion, pred[2,1024,512]{1,2,0:T(8,128)(4,1)S(1)} %iota_compare_fusion), kind=kOutput, calls=%fused_computation.19 | convolution fusion | flops 3228041216 | bytes 12615680 | tf_op jit(solution)/shard_map/bkrn,bnkd->bkrd/dot_general | solution.py:21
  113.3 1.5 copy.141
  114.8 130.5 %all-reduce.2.cloned.1.call-done = f32[8,2,256,2,128]{4,2,3,0,1:T(8,128)} async-done(((f32[8,2,256,2,128]{4,2,3,0,1:T(8,128)}), f32[8,2,256,2,128]{4,2,3,0,1:T(8,128)}) %all-reduce.2.cloned.1.call-update) | async-done | bytes 4194320 | tf_op jit(solution)/shard_map/psum | solution.py:13
  245.2 4.1 %fusion.30 = (f32[8,2,64]{2,1,0:T(2,128)S(1)}, f32[8,2,64,256]{3,2,1,0:T(8,128)S(1)}) fusion(f32[8,2,64,128]{3,2,1,0:T(8,128)} %bitcast.142, f32[8,2,256,2,128]{4,2,3,0,1:T(8,128)} %all-reduce.2.cloned.1.call-done, pred[8,64,256]{2,1,0:T(8,128)(4,1)S(1)} %broadcast_compare_fusion), kind=kOutput, calls=%fused_computation.62 | convolution fusion | flops 403438592 | bytes 3805184 | tf_op jit(solution)/shard_map/bkrd,bnkd->bkrn/dot_general | solution.py:36
  249.4 0.4 fusion.19
  249.8 0.1 reshape.223
  250.0 0.1 reshape.224
  250.1 0.7 reshape.235
  250.8 3.2 %all-to-all-start.2 = ((f32[2,1,512]{2,1,0:T(1,128)}), f32[2,1,512]{2,1,0:T(1,128)S(1)}, u32[]{:S(2)}, u32[]{:S(2)}) async-start(f32[2,1,512]{2,1,0:T(1,128)} %reshape.235), calls=%async_computation.2 | async-start | bytes 8192 | tf_op jit(solution)/shard_map/all_to_all | solution.py:122
  254.0 0.1 max_broadcast_in_dim.26
  254.2 0.1 reshape.216
  254.3 0.7 reshape.233
  255.0 2.8 all-to-all-done.2
  257.8 3.2 %all-to-all-start.1 = ((f32[2,1,512]{2,1,0:T(1,128)}), f32[2,1,512]{2,1,0:T(1,128)S(1)}, u32[]{:S(2)}, u32[]{:S(2)}) async-start(f32[2,1,512]{2,1,0:T(1,128)} %reshape.233), calls=%async_computation.1 | async-start | bytes 8192 | tf_op jit(solution)/shard_map/all_to_all | solution.py:121
  261.0 3.3 %fusion.7 = f32[8,2,64,128]{3,2,1,0:T(8,128)S(1)} fusion(f32[8,2,256,2,128]{4,2,3,0,1:T(8,128)} %all-reduce.2.cloned.1.call-done, f32[8,2,64,256]{3,2,1,0:T(8,128)S(1)} %get-tuple-element.19, f32[8,2,64]{2,1,0:T(2,128)S(1)} %broadcast_maximum_fusion.1), kind=kOutput, calls=%fused_computation.11 | convolution fusion | flops 402915328 | bytes 3674112 | tf_op jit(solution)/shard_map/bkrn,bnkd->bkrd/dot_general | solution.py:21
  264.3 0.8 copy.142
  265.2 0.6 broadcast.71
  265.8 0.7 reduce.6
  266.5 0.1 reshape.236
  266.6 3.5 %all-to-all-start = ((f32[2,8,1,4,16,128]{5,4,3,1,2,0:T(8,128)}), f32[2,8,1,4,16,128]{5,4,3,1,2,0:T(8,128)S(1)}, u32[]{:S(2)}, u32[]{:S(2)}) async-start(f32[2,8,1,4,16,128]{5,4,3,1,2,0:T(8,128)} %bitcast.137), calls=%async_computation | async-start | bytes 1048576 | tf_op jit(solution)/shard_map/all_to_all | solution.py:123
  270.1 0.7 reduce.5
  270.8 0.1 reshape.234
  270.9 0.1 reshape.218
  271.0 0.1 fusion.23
  271.1 0.1 reshape.225
  271.3 5.9 %all-to-all-done = f32[2,8,1,4,16,128]{5,4,3,1,2,0:T(8,128)S(1)} async-done(((f32[2,8,1,4,16,128]{5,4,3,1,2,0:T(8,128)}), f32[2,8,1,4,16,128]{5,4,3,1,2,0:T(8,128)S(1)}, u32[]{:S(2)}, u32[]{:S(2)}) %all-to-all-start) | async-done | bytes 524320 | tf_op jit(solution)/shard_map/all_to_all | solution.py:123
  277.1 0.2 multiply_reduce_fusion
  277.3 0.7 fusion.16
  278.0 0.7 copy.143
  (35 shorter events, 0.6 us)
Async XLA Ops:
  7.2 78.8 %copy-start = (f32[2,128,16,128]{3,2,1,0:T(8,128)S(1)}, f32[2,128,16,128]{3,2,1,0:T(8,128)}, u32[]{:S(2)}) copy-start(f32[2,128,16,128]{3,2,1,0:T(8,128)} %param.7) | copy-start | bytes 6291460
  7.2 40.2 %all-gather.6.cloned.1.call-start = ((), (), s32[]{:S(2)}) async-start(), calls=%async_computation.4 | async-start | bytes 5242880 | tf_op jit(solution)/shard_map/all_gather | solution.py:94
  9.7 76.3 %all-gather.4.cloned.1.call-start = ((), (), s32[]{:S(2)}) async-start(), calls=%async_computation.3 | async-start | bytes 3145728 | tf_op jit(solution)/shard_map/all_gather | solution.py:84
  10.4 234.8 %all-reduce.2.cloned.1.call-start = ((), (), s32[]{:S(2)}) async-start(), calls=%async_computation.5 | async-start | bytes 8388608 | tf_op jit(solution)/shard_map/psum | solution.py:13
  52.0 0.7 copy-start.5
  52.0 5.1 %copy-start.4 = (s32[8]{0:T(128)S(1)}, s32[8]{0:T(128)}, u32[]{:S(2)}) copy-start(s32[8]{0:T(128)} %param.10) | copy-start | bytes 100
  52.0 5.5 %copy-start.1 = (f32[8,1,4,16,128]{4,3,2,1,0:T(8,128)S(1)}, f32[8,1,4,16,128]{4,3,2,1,0:T(8,128)}, u32[]{:S(2)}) copy-start(f32[8,1,4,16,128]{4,3,2,1,0:T(8,128)} %param.8) | copy-start | bytes 786436
  52.0 19.0 %copy-start.3 = (f32[8,1,4,2,2,128]{5,4,3,2,1,0:T(2,128)S(1)}, f32[8,1,4,2,2,128]{5,4,3,2,1,0:T(2,128)}, u32[]{:S(2)}) copy-start(f32[8,1,4,2,2,128]{5,4,3,2,1,0:T(2,128)} %param.9) | copy-start | bytes 196612
  95.6 2.2 copy-start.2
  250.8 7.0 %all-to-all-start.2 = ((f32[2,1,512]{2,1,0:T(1,128)}), f32[2,1,512]{2,1,0:T(1,128)S(1)}, u32[]{:S(2)}, u32[]{:S(2)}) async-start(f32[2,1,512]{2,1,0:T(1,128)} %reshape.235), calls=%async_computation.2 | async-start | bytes 8192 | tf_op jit(solution)/shard_map/all_to_all | solution.py:122
  257.8 8.8 %all-to-all-start.1 = ((f32[2,1,512]{2,1,0:T(1,128)}), f32[2,1,512]{2,1,0:T(1,128)S(1)}, u32[]{:S(2)}, u32[]{:S(2)}) async-start(f32[2,1,512]{2,1,0:T(1,128)} %reshape.233), calls=%async_computation.1 | async-start | bytes 8192 | tf_op jit(solution)/shard_map/all_to_all | solution.py:121
  266.6 10.6 %all-to-all-start = ((f32[2,8,1,4,16,128]{5,4,3,1,2,0:T(8,128)}), f32[2,8,1,4,16,128]{5,4,3,1,2,0:T(8,128)S(1)}, u32[]{:S(2)}, u32[]{:S(2)}) async-start(f32[2,8,1,4,16,128]{5,4,3,1,2,0:T(8,128)} %bitcast.137), calls=%async_computation | async-start | bytes 1048576 | tf_op jit(solution)/shard_map/all_to_all | solution.py:123
Sparse Core Ops, SparseCore 0:
  10.2 37.1 all-gather.5
  49.5 36.4 all-gather.3
  88.4 156.8 all-reduce.1
where the time goes:
time: 286 us; the launch traced here: 285 us
  waiting for transfers between devices  187 us (65%)
  matrix products  36.7 us (13%)
  blocking collectives  16.8 us (6%)
  between operations  14 us (5%)
  local copies, waits for them, and re-layouts  10.3 us (4%)
  starting transfers between devices  10 us (3%)
  other arithmetic  10 us (3%)
    psum x1, waiting for transfers between devices, broadcast(): return lax.psum(kept, axis)  130 us
    all_gather x1, waiting for transfers between devices, on_device(): all_requests = lax.all_gather(kv_cache, 'head', axis=0, tiled=True)  36.9 us
    dot_general x2, matrix products, online_fold(): new_acc = jnp.einsum(pattern, weights, value_rows, precision=HIGH_PRECISION)  18.8 us
    dot_general x2, matrix products, block_fold(): jnp.einsum('bkrd,bnkd->bkrn', query_rows, key_block[:, 0], precision=HIGH...  13.7 us
    all_gather x1, blocking collectives, on_device(): lax.all_gather(decode_q, 'ctx', axis=1, tiled=True)  12.6 us
    all_gather x1, waiting for transfers between devices, on_device(): lax.all_gather(kv_cache, 'ctx', axis=2, tiled=True)  10.6 us
    all_to_all x1, waiting for transfers between devices, on_device(): lax.all_to_all(shaped[2], 'ctx', split_axis=0, concat_axis=0, tiled=True)  5.85 us
  transfers between devices with their start and end apart: 6, of which 5 were waited for; matrix products, arithmetic and copies ran while one was open for 16% of the time, Pallas kernels for 0%

commit v1 on v0

--- a/solution.py
+++ b/solution.py
@@ -6,6 +6,28 @@
 
 NEG_FILL = -1e30
 HIGH_PRECISION = lax.Precision.HIGHEST
+
+
+def joined_along(blocks, dim):
+    dims = list(blocks.shape[1:])
+    dims[dim] *= blocks.shape[0]
+    return jnp.moveaxis(blocks, 0, dim).reshape(dims)
+
+
+def ring_gather(x, axis, dim):
+    length = lax.axis_size(axis)
+    pairs = [(i, (i + 1) % length) for i in range(length)]
+    back = [(b, a) for a, b in pairs]
+    lower, upper = ([], [])
+    for step in range(length - 1):
+        if step % 2 == 0:
+            lower.append(lax.ppermute(lower[-1] if lower else x, axis, pairs))
+        else:
+            upper.append(lax.ppermute(upper[-1] if upper else x, axis, back))
+    tiles = jnp.stack([*lower[::-1], x, *upper])
+    shift = lax.axis_index(axis) - len(lower)
+    tiles = tiles[(jnp.arange(length) - shift) % length]
+    return joined_along(tiles, dim)
 
 
 def broadcast(value, axis, source):
@@ -91,7 +113,7 @@
     prefill_out = jnp.transpose(
         prefill_vals.reshape(req_group, rep_kv, span_rows, group_size, head_dim), (0, 2, 1, 3, 4)
     ).reshape(prefill_q.shape)
-    all_requests = lax.all_gather(kv_cache, "head", axis=0, tiled=True)
+    all_requests = ring_gather(kv_cache, "head", 0)
     head_cache = broadcast(all_requests, "rep", head_index)
     requests, row_count, step_count, local_heads, unused_dim = decode_q.shape
     kv_heads = local_heads // group_size

time: 286 us -> 272 us (0.951); the launches traced: 285 us -> 266 us
  waiting for transfers between devices: 187 us -> 148 us
  local copies, waits for them, and re-layouts: 10.3 us -> 22 us
  starting transfers between devices: 10 us -> 15.2 us
  other arithmetic: 10 us -> 14.7 us
  blocking collectives: 16.8 us -> 13 us
    all_gather x1 -> x0, waiting for transfers between devices: 36.9 us -> none  [on_device(): all_requests = lax.all_gather(kv_cache, 'head', axis=0, tiled=True)]
    ppermute x0 -> x3, waiting for transfers between devices: none -> 30.5 us  [the longest x2 30.5 us: ring_gather(): lower.append(lax.ppermute(lower[-1] if lower else x, axis, pairs))]
    psum x1, waiting for transfers between devices: 130 us -> 109 us  [broadcast(): return lax.psum(kept, axis)]
    all_gather x1, waiting for transfers between devices: 10.6 us -> 0.02 us  [on_device(): lax.all_gather(kv_cache, 'ctx', axis=2, tiled=True)]
    gather x0 -> x1, local copies, waits for them, and re-layouts: none -> 8.38 us  [ring_gather(): tiles = tiles[(jnp.arange(length) - shift) % length]]
    another operation x0 -> x1, other arithmetic: none -> 5.27 us  [ring_gather(): tiles = jnp.stack([*lower[::-1], x, *upper])]
    ppermute x0 -> x3, starting transfers between devices: none -> 5.14 us  [the longest x2 3.12 us: ring_gather(): lower.append(lax.ppermute(lower[-1] if lower else x, axis, pairs))]
    all_gather x1, blocking collectives: 12.6 us -> 7.76 us  [on_device(): lax.all_gather(decode_q, 'ctx', axis=1, tiled=True)]
  transfers between devices with their start and end apart: 6 -> 8, of which waited for: 5 -> 5; matrix products, arithmetic and copies ran while one was open for 16% -> 25% of each run, Pallas kernels for 0% -> 0%
where the time goes in v1:
time: 272 us; the launch traced here: 266 us
  waiting for transfers between devices  148 us (54%)
  matrix products  37.3 us (14%)
  local copies, waits for them, and re-layouts  22 us (8%)
  between operations  16 us (6%)
  starting transfers between devices  15.2 us (6%)
  other arithmetic  14.7 us (5%)
  blocking collectives  13 us (5%)
    psum x1, waiting for transfers between devices, broadcast(): return lax.psum(kept, axis)  109 us
    ppermute x2, waiting for transfers between devices, ring_gather(): lower.append(lax.ppermute(lower[-1] if lower else x, axis, pairs))  30.5 us
    dot_general x2, matrix products, online_fold(): new_acc = jnp.einsum(pattern, weights, value_rows, precision=HIGH_PRECISION)  19.4 us
    dot_general x2, matrix products, block_fold(): jnp.einsum('bkrd,bnkd->bkrn', query_rows, key_block[:, 0], precision=HIGH...  13.7 us
    gather x1, local copies, waits for them, and re-layouts, ring_gather(): tiles = tiles[(jnp.arange(length) - shift) % length]  8.38 us
    all_gather x1, blocking collectives, on_device(): lax.all_gather(decode_q, 'ctx', axis=1, tiled=True)  7.76 us
    all_to_all x1, waiting for transfers between devices, on_device(): lax.all_to_all(shaped[2], 'ctx', split_axis=0, concat_axis=0, tiled=True)  5.84 us
  transfers between devices with their start and end apart: 8, of which 5 were waited for; matrix products, arithmetic and copies ran while one was open for 25% of the time, Pallas kernels for 0%

profile of v1, /device:TPU:0, one launch (start us, length us, event | category | flops | bytes accessed | tf_op | source)
XLA Modules:
  0.0 266.4 jit_solution(17719665800390421692)
XLA Ops:
  8.1 0.5 collective-permute-start
  8.6 2.0 collective-permute-start.2
  10.6 21.2 %collective-permute-done = f32[2,2,256,2,128]{4,3,2,1,0:T(2,128)S(1)} collective-permute-done((f32[2,2,256,2,128]{4,3,2,1,0:T(2,128)}, f32[2,2,256,2,128]{4,3,2,1,0:T(2,128)S(1)}, u32[]{:S(2)}, u32[]{:S(2)}) %collective-permute-start) | collective-permute-done | bytes 1048608 | tf_op jit(solution)/shard_map/ppermute | solution.py:24
  31.8 2.6 collective-permute-start.1
  34.4 2.3 copy.82
  36.8 9.3 %collective-permute-done.1 = f32[2,2,256,2,128]{4,3,2,1,0:T(2,128)} collective-permute-done((f32[2,2,256,2,128]{4,3,2,1,0:T(2,128)S(1)}, f32[2,2,256,2,128]{4,3,2,1,0:T(2,128)}, u32[]{:S(2)}, u32[]{:S(2)}) %collective-permute-start.1) | collective-permute-done | bytes 1048608 | tf_op jit(solution)/shard_map/ppermute | solution.py:24
  46.1 5.3 %pad_maximum_fusion = f32[4,2,2,256,2,128]{5,4,3,2,1,0:T(2,128)} fusion(f32[1,2,2,256,2,128]{5,4,3,2,1,0:T(2,128)} %bitcast.14, f32[1,2,2,256,2,128]{5,4,3,2,1,0:T(2,128)} %bitcast.147, f32[1,2,2,256,2,128]{5,4,3,2,1,0:T(2,128)S(1)} %bitcast.152, f32[1,2,2,256,2,128]{5,4,3,2,1,0:T(2,128)} %bitcast.11), kind=kLoop, calls=%fused_computation.6 | loop fusion | flops 3145728 | bytes 8388608 | tf_op jit(solution)/shard_map/stack | solution.py:27
  51.4 8.4 %gather_fusion = f32[4,2,2,256,2,128]{5,4,3,2,1,0:T(2,128)} fusion(f32[4,2,2,256,2,128]{5,4,3,2,1,0:T(2,128)} %pad_maximum_fusion, s32[1024]{0:T(1024)S(1)} %pad_clamp_fusion), kind=kCustom, calls=%fused_computation | custom fusion | bytes 8388624 | tf_op jit(solution)/shard_map/gather | solution.py:29
  59.8 4.1 %broadcast_select_fusion = f32[4,2,2,256,2,128]{5,4,3,2,1,0:T(2,128)S(1)} fusion(f32[4,2,2,256,2,128]{5,4,3,2,1,0:T(2,128)} %gather_fusion, pred[]{:T(512)S(6)} %eq.5), kind=kLoop, calls=%fused_computation.11 | loop fusion | flops 1048576 | bytes 8388609 | tf_op jit(solution)/shard_map/jit(_where)/select_n | solution.py:34
  63.8 2.5 copy.86
  66.4 0.6 copy-done.5
  67.0 5.2 %all-gather = s32[2,1,8]{2,1,0:T(1,128)S(1)} all-gather(s32[1,1,8]{2,1,0:T(1,128)S(1)} %bitcast.157), channel_id=1, replica_groups=mesh['ctx'=2,'head'=4,'rep'=4] {'ctx'}, dimensions={0}, use_global_device_ids=true | all-gather | bytes 96 | tf_op jit(solution)/shard_map/all_gather | solution.py:122
  72.4 0.1 broadcast_in_dim.48
  72.5 0.1 le.37
  72.6 7.8 %all_gather.11 = f32[8,2,4,16,128]{4,3,2,1,0:T(8,128)S(1)} all-gather(f32[8,1,4,16,128]{4,3,2,1,0:T(8,128)S(1)} %copy-done.1), channel_id=1, replica_groups=mesh['ctx'=2,'head'=4,'rep'=4] {'ctx'}, dimensions={1}, use_global_device_ids=true | all-gather | bytes 786432 | tf_op jit(solution)/shard_map/all_gather | solution.py:121
  80.4 0.9 copy.87
  81.4 0.1 lt.40
  81.6 0.1 broadcast_compare_fusion
  81.7 3.6 %fusion.33 = (f32[8,4,2,8]{3,1,2,0:T(4,128)S(1)}, f32[8,1,4,2,8,4]{4,5,2,3,0,1:T(4,128)S(1)}) fusion(f32[8,1,4,1,2,128]{5,4,3,2,1,0:T(2,128)S(1)} %get-tuple-element.13, pred[4,4]{1,0:T(4,128)(4,1)S(1)} %iota_compare_fusion.1, f32[8,1,4,16,128]{4,3,2,1,0:T(8,128)S(1)} %copy-done.1), kind=kOutput, calls=%fused_computation.72 | convolution fusion | flops 3151360 | bytes 305168 | tf_op jit(solution)/shard_map/artkgd,arskd->artkgs/dot_general | solution.py:153
  85.3 0.6 iota_compare_fusion
  86.0 9.6 %fusion = (f32[2,2,1024]{2,1,0:T(2,128)S(1)}, f32[2,2,1024,512]{2,3,1,0:T(8,128)S(1)}) fusion(pred[2,1024,512]{1,2,0:T(8,128)(4,1)S(1)} %iota_compare_fusion, f32[2,2,512,2,128]{4,2,3,0,1:T(8,128)} %all-gather.3.cloned.1.call-done, f32[2,128,16,128]{3,2,1,0:T(8,128)S(1)} %copy-done), kind=kOutput, calls=%fused_computation.3 | convolution fusion | flops 3227512832 | bytes 12599296 | tf_op jit(solution)/shard_map/bkrd,bnkd->bkrn/dot_general | solution.py:58
  95.6 2.2 fusion.1
  97.8 15.4 %divide_bitcast_fusion = f32[2,128,2,8,128]{4,3,1,2,0:T(8,128)S(1)} fusion(f32[2,2,1024]{2,1,0:T(2,128)S(1)} %fusion.1, f32[2,2,512,2,128]{4,2,3,0,1:T(8,128)S(1)} %copy-done.2, f32[2,2,1024,512]{2,3,1,0:T(8,128)S(1)} %get-tuple-element.17, f32[2,2,1024]{2,1,0:T(2,128)S(1)} %broadcast_maximum_fusion, pred[2,1024,512]{1,2,0:T(8,128)(4,1)S(1)} %iota_compare_fusion), kind=kOutput, calls=%fused_computation.21 | convolution fusion | flops 3228041216 | bytes 12615680 | tf_op jit(solution)/shard_map/bkrn,bnkd->bkrd/dot_general | solution.py:43
  113.3 1.5 copy.141
  114.7 109.3 %all-reduce.2.cloned.1.call-done = f32[8,2,256,2,128]{4,2,3,0,1:T(8,128)} async-done(((f32[8,2,256,2,128]{4,2,3,0,1:T(8,128)}), f32[8,2,256,2,128]{4,2,3,0,1:T(8,128)}) %all-reduce.2.cloned.1.call-update) | async-done | bytes 4194320 | tf_op jit(solution)/shard_map/psum | solution.py:35
  224.1 4.1 %fusion.32 = (f32[8,2,64]{2,1,0:T(2,128)S(1)}, f32[8,2,64,256]{3,2,1,0:T(8,128)S(1)}) fusion(f32[8,2,64,128]{3,2,1,0:T(8,128)} %bitcast.151, f32[8,2,256,2,128]{4,2,3,0,1:T(8,128)} %all-reduce.2.cloned.1.call-done, pred[8,64,256]{2,1,0:T(8,128)(4,1)S(1)} %broadcast_compare_fusion), kind=kOutput, calls=%fused_computation.71 | convolution fusion | flops 403438592 | bytes 3805184 | tf_op jit(solution)/shard_map/bkrd,bnkd->bkrn/dot_general | solution.py:58
  228.3 0.1 max_broadcast_in_dim.26
  228.4 0.1 reshape.269
  228.5 0.7 reshape.294
  229.2 3.2 %all-to-all-start.1 = ((f32[2,1,512]{2,1,0:T(1,128)}), f32[2,1,512]{2,1,0:T(1,128)S(1)}, u32[]{:S(2)}, u32[]{:S(2)}) async-start(f32[2,1,512]{2,1,0:T(1,128)} %reshape.294), calls=%async_computation.1 | async-start | bytes 8192 | tf_op jit(solution)/shard_map/all_to_all | solution.py:143
  232.4 0.4 fusion.19
  232.9 0.1 reshape.276
  233.0 0.1 reshape.277
  233.1 4.0 %fusion.7 = f32[8,2,64,128]{3,2,1,0:T(8,128)} fusion(f32[8,2,256,2,128]{4,2,3,0,1:T(8,128)} %all-reduce.2.cloned.1.call-done, f32[8,2,64,256]{3,2,1,0:T(8,128)S(1)} %get-tuple-element.19, f32[8,2,64]{2,1,0:T(2,128)S(1)} %broadcast_maximum_fusion.1), kind=kOutput, calls=%fused_computation.14 | convolution fusion | flops 402915328 | bytes 3674112 | tf_op jit(solution)/shard_map/bkrn,bnkd->bkrd/dot_general | solution.py:43
  237.1 0.7 reshape.296
  237.8 1.9 copy.142
  239.7 3.3 %all-to-all-start.2 = ((f32[2,1,512]{2,1,0:T(1,128)}), f32[2,1,512]{2,1,0:T(1,128)S(1)}, u32[]{:S(2)}, u32[]{:S(2)}) async-start(f32[2,1,512]{2,1,0:T(1,128)} %reshape.296), calls=%async_computation.2 | async-start | bytes 8192 | tf_op jit(solution)/shard_map/all_to_all | solution.py:144
  242.9 0.5 broadcast.144
  243.4 0.7 reduce.5
  244.2 0.1 reshape.271
  244.3 2.4 all-to-all-done.2
  246.7 3.5 %all-to-all-start = ((f32[2,8,1,4,16,128]{5,4,3,1,2,0:T(8,128)}), f32[2,8,1,4,16,128]{5,4,3,1,2,0:T(8,128)S(1)}, u32[]{:S(2)}, u32[]{:S(2)}) async-start(f32[2,8,1,4,16,128]{5,4,3,1,2,0:T(8,128)} %bitcast.144), calls=%async_computation | async-start | bytes 1048576 | tf_op jit(solution)/shard_map/all_to_all | solution.py:145
  250.2 0.7 reduce.6
  251.0 0.1 fusion.23
  251.3 5.8 %all-to-all-done = f32[2,8,1,4,16,128]{5,4,3,1,2,0:T(8,128)S(1)} async-done(((f32[2,8,1,4,16,128]{5,4,3,1,2,0:T(8,128)}), f32[2,8,1,4,16,128]{5,4,3,1,2,0:T(8,128)S(1)}, u32[]{:S(2)}, u32[]{:S(2)}) %all-to-all-start) | async-done | bytes 524320 | tf_op jit(solution)/shard_map/all_to_all | solution.py:145
  257.1 0.2 multiply_reduce_fusion
  257.4 0.7 fusion.16
  258.0 0.7 copy.143
  (43 shorter events, 1.0 us)
Async XLA Ops:
  8.0 78.0 %copy-start = (f32[2,128,16,128]{3,2,1,0:T(8,128)S(1)}, f32[2,128,16,128]{3,2,1,0:T(8,128)}, u32[]{:S(2)}) copy-start(f32[2,128,16,128]{3,2,1,0:T(8,128)} %param.7) | copy-start | bytes 6291460
  8.0 78.0 %all-gather.3.cloned.1.call-start = ((), (), s32[]{:S(2)}) async-start(), calls=%async_computation.3 | async-start | bytes 3145728 | tf_op jit(solution)/shard_map/all_gather | solution.py:106
  8.1 23.7 %collective-permute-start = (f32[2,2,256,2,128]{4,3,2,1,0:T(2,128)}, f32[2,2,256,2,128]{4,3,2,1,0:T(2,128)S(1)}, u32[]{:S(2)}, u32[]{:S(2)}) collective-permute-start(f32[2,2,256,2,128]{4,3,2,1,0:T(2,128)} %param.6), channel_id=1, source_target_pairs={{0,4},{4,8},{8,12},{12,0},{1,5},{5,9},{9,13},{13,1},{2,6},{6,10},{... | collective-permute-start | bytes 3145736 | tf_op jit(solution)/shard_map/ppermute | solution.py:24
  8.6 28.2 %collective-permute-start.2 = (f32[2,2,256,2,128]{4,3,2,1,0:T(2,128)}, f32[2,2,256,2,128]{4,3,2,1,0:T(2,128)}, u32[]{:S(2)}, u32[]{:S(2)}) collective-permute-start(f32[2,2,256,2,128]{4,3,2,1,0:T(2,128)} %param.6), channel_id=1, source_target_pairs={{4,0},{8,4},{12,8},{0,12},{5,1},{9,5},{13,9},{1,13},{6,2},{10,6},{... | collective-permute-start | bytes 3145736 | tf_op jit(solution)/shard_map/ppermute | solution.py:26
  31.8 14.3 %collective-permute-start.1 = (f32[2,2,256,2,128]{4,3,2,1,0:T(2,128)S(1)}, f32[2,2,256,2,128]{4,3,2,1,0:T(2,128)}, u32[]{:S(2)}, u32[]{:S(2)}) collective-permute-start(f32[2,2,256,2,128]{4,3,2,1,0:T(2,128)S(1)} %collective-permute-done), channel_id=1, source_target_pairs={{0,4},{4,8},{8,12},{12,0},{1,5},{5,9},{9,13},{13,1},{2,6},{6,10},{... | collective-permute-start | bytes 3145736 | tf_op jit(solution)/shard_map/ppermute | solution.py:24
  36.7 187.4 %all-reduce.2.cloned.1.call-start = ((), (), s32[]{:S(2)}) async-start(), calls=%async_computation.4 | async-start | bytes 8388608 | tf_op jit(solution)/shard_map/psum | solution.py:35
  66.4 0.7 copy-start.5
  66.4 5.9 %copy-start.4 = (s32[8]{0:T(128)S(1)}, s32[8]{0:T(128)}, u32[]{:S(2)}) copy-start(s32[8]{0:T(128)} %param.10) | copy-start | bytes 100
  66.4 6.2 %copy-start.1 = (f32[8,1,4,16,128]{4,3,2,1,0:T(8,128)S(1)}, f32[8,1,4,16,128]{4,3,2,1,0:T(8,128)}, u32[]{:S(2)}) copy-start(f32[8,1,4,16,128]{4,3,2,1,0:T(8,128)} %param.8) | copy-start | bytes 786436
  66.4 15.2 %copy-start.3 = (f32[8,1,4,2,2,128]{5,4,3,2,1,0:T(2,128)S(1)}, f32[8,1,4,2,2,128]{5,4,3,2,1,0:T(2,128)}, u32[]{:S(2)}) copy-start(f32[8,1,4,2,2,128]{5,4,3,2,1,0:T(2,128)} %param.9) | copy-start | bytes 196612
  95.6 2.2 copy-start.2
  229.2 10.4 %all-to-all-start.1 = ((f32[2,1,512]{2,1,0:T(1,128)}), f32[2,1,512]{2,1,0:T(1,128)S(1)}, u32[]{:S(2)}, u32[]{:S(2)}) async-start(f32[2,1,512]{2,1,0:T(1,128)} %reshape.294), calls=%async_computation.1 | async-start | bytes 8192 | tf_op jit(solution)/shard_map/all_to_all | solution.py:143
  239.7 7.1 %all-to-all-start.2 = ((f32[2,1,512]{2,1,0:T(1,128)}), f32[2,1,512]{2,1,0:T(1,128)S(1)}, u32[]{:S(2)}, u32[]{:S(2)}) async-start(f32[2,1,512]{2,1,0:T(1,128)} %reshape.296), calls=%async_computation.2 | async-start | bytes 8192 | tf_op jit(solution)/shard_map/all_to_all | solution.py:144
  246.7 10.4 %all-to-all-start = ((f32[2,8,1,4,16,128]{5,4,3,1,2,0:T(8,128)}), f32[2,8,1,4,16,128]{5,4,3,1,2,0:T(8,128)S(1)}, u32[]{:S(2)}, u32[]{:S(2)}) async-start(f32[2,8,1,4,16,128]{5,4,3,1,2,0:T(8,128)} %bitcast.144), calls=%async_computation | async-start | bytes 1048576 | tf_op jit(solution)/shard_map/all_to_all | solution.py:145
Sparse Core Ops, SparseCore 0:
  36.8 34.7 all-gather.2
Sparse Core Ops, SparseCore 1:
  66.5 157.6 all-reduce.1
